TPU v7x, 512 devices: a whole 4x8x8 slice. The times are simulated.
512 devices in a mesh: depth: 4 (over x), row: 16 (over y, core), col: 8 (over z).
Axes of the slice: x: 4, y: 8, z: 8, core: 2. Of those that a mesh axis runs over, the one named last changes fastest.
Arguments:
- latents: bfloat16 [4, 16, 8, 3, 8, 8, 8, 256], P('depth', 'row', 'col'), may hold values from -6 to 6
- neighbours: int32 [4, 16, 8, 3, 6], P('depth', 'row', 'col'), may hold values from -1 to 1535, as said below
- owners: int32 [4, 16, 8, 3, 8], P('depth', 'row', 'col'), may hold values from -1 to 255, as said below
- conv_weight: bfloat16 [27, 256, 256], P(None, None, 'row'), may hold values from -0.078125 to 0.078125
- step_embed: float32 [256], replicated, may hold values from -6 to 6
- up_weight: bfloat16 [8, 256, 128], replicated, may hold values from -0.375 to 0.375
Outputs:
- upsampled: bfloat16 [4, 16, 8, 16, 8, 8, 8, 128], P('depth', 'row', 'col')
Inputs may be any that keep to these rules, and one draw needn't show every extreme that they name: `neighbours`: entry d names the brick beside a brick's face in direction d (order -z, +z, -y, +y, -x, +x) as ((depth * 16 + row) * 8 + col) * 3 + slot; that brick lies on the same device or on the device beside it across that face. -1 where no brick is there and in every entry of an empty slot. The occupied slots of a device come first. `owners`: for an occupied slot, entry k is j * 16 + u: child k goes to slot u of the device at row j with the same depth and col; -1 in empty slots. Each device holds 1 to 3 occupied slots, and in every line of devices along row some device holds 3. Every device receives exactly 16 children, each slot once, and no device sends more than 2 children to one device.
All inputs are finite; a program needn't handle non-finite values.
Results may differ from a plain program's by a relative error of at most 0.0051.
Values may be sent and summed in bfloat16 or wider, within the bound.
No kernel may reach another device: no remote copies, remote signals or barrier semaphores. Data moves between devices by JAX's collectives and lax.ppermute only.
A program may use at most 64 MiB of HBM per device.

v0:
```python
import jax
import jax.numpy as jnp
from jax import lax
from jax.sharding import PartitionSpec as P

OCAP = 16


def with_halo(cells, sides, width):
    for axis, dim in sides:
        count = lax.axis_size(axis)
        ends = count - 1
        head = lax.slice_in_dim(cells, 0, width, axis=dim)
        tail = lax.slice_in_dim(cells, cells.shape[dim] - width, cells.shape[dim], axis=dim)
        cells = jnp.concatenate(
            [
                lax.ppermute(tail, axis, [(i, (i + 1) % count) for i in range(ends)]),
                cells,
                lax.ppermute(head, axis, [((i + 1) % count, i) for i in range(ends)]),
            ],
            axis=dim,
        )
    return cells


def normed_silu(values):
    mean_square = jnp.mean(values * values, axis=-1, keepdims=True)
    return jax.nn.silu(values * lax.rsqrt(mean_square + 1e-06))


def borrowed(local_face, remote_face, near_index, own_index, offset, slots_dev):
    owner_dev = near_index // slots_dev
    in_slot = near_index % slots_dev
    chosen = jnp.where(
        near_index < 0,
        -1,
        jnp.where(
            owner_dev == own_index,
            in_slot,
            jnp.where(owner_dev == own_index + offset, slots_dev + in_slot, -1),
        ),
    )
    picker = (chosen[:, None] == jnp.arange(2 * slots_dev, dtype=jnp.int32)[None, :]).astype(
        jnp.bfloat16
    )
    stacked = jnp.concatenate([local_face, remote_face], axis=0).reshape(2 * slots_dev, -1)
    picked = jnp.dot(picker, stacked, preferred_element_type=jnp.float32)
    return picked.astype(jnp.bfloat16).reshape(local_face.shape)


def padded_field(source, near_ids, own_index, row_count, col_count):
    slots_dev = source.shape[0]
    edge_len = source.shape[1]
    depth_faces = with_halo(jnp.stack([source[:, 0], source[:, -1]]), (("depth", 0),), 1)
    row_faces = with_halo(jnp.stack([source[:, :, 0], source[:, :, -1]]), (("row", 0),), 1)
    col_faces = with_halo(jnp.stack([source[:, :, :, 0], source[:, :, :, -1]]), (("col", 0),), 1)
    plane_size = row_count * col_count
    below_z = borrowed(
        depth_faces[2], depth_faces[0], near_ids[:, 0], own_index, -plane_size, slots_dev
    )
    above_z = borrowed(
        depth_faces[1], depth_faces[3], near_ids[:, 1], own_index, plane_size, slots_dev
    )
    below_y = borrowed(row_faces[2], row_faces[0], near_ids[:, 2], own_index, -col_count, slots_dev)
    above_y = borrowed(row_faces[1], row_faces[3], near_ids[:, 3], own_index, col_count, slots_dev)
    below_x = borrowed(col_faces[2], col_faces[0], near_ids[:, 4], own_index, -1, slots_dev)
    above_x = borrowed(col_faces[1], col_faces[3], near_ids[:, 5], own_index, 1, slots_dev)
    padded = jnp.zeros(
        (slots_dev, edge_len + 2, edge_len + 2, edge_len + 2, source.shape[-1]), jnp.bfloat16
    )
    padded = padded.at[:, 1:-1, 1:-1, 1:-1].set(source)
    padded = padded.at[:, 0, 1:-1, 1:-1].set(below_z)
    padded = padded.at[:, edge_len + 1, 1:-1, 1:-1].set(above_z)
    padded = padded.at[:, 1:-1, 0, 1:-1].set(below_y)
    padded = padded.at[:, 1:-1, edge_len + 1, 1:-1].set(above_y)
    padded = padded.at[:, 1:-1, 1:-1, 0].set(below_x)
    padded = padded.at[:, 1:-1, 1:-1, edge_len + 1].set(above_x)
    return padded


def convolve(source, weight, near_ids, own_index, row_count, col_count):
    channels = source.shape[-1]
    padded = padded_field(source, near_ids, own_index, row_count, col_count)
    weight_piece = lax.all_gather(weight, "row", axis=2, tiled=True)
    kernel = weight_piece.reshape(3, 3, 3, channels, weight_piece.shape[2])
    return lax.conv_general_dilated(
        padded,
        kernel,
        (1, 1, 1),
        "VALID",
        dimension_numbers=("NDHWC", "DHWIO", "NDHWC"),
        preferred_element_type=jnp.float32,
    )


def body(latents, neighbours, owners, conv_weight, step_embed, up_weight):
    row_count = lax.axis_size("row")
    col_count = lax.axis_size("col")
    own_row = lax.axis_index("row")
    own_index = (lax.axis_index("depth") * row_count + own_row) * col_count + lax.axis_index("col")
    latent = latents.reshape(latents.shape[3:]).astype(jnp.float32)
    slots_dev, edge_len, channels = (latent.shape[0], latent.shape[1], latent.shape[-1])
    half_len = edge_len // 2
    out_channels = up_weight.shape[-1]
    near_ids = neighbours.reshape(slots_dev, 6)
    owner_ids = owners.reshape(slots_dev * 8)
    first_input = normed_silu(latent).astype(jnp.bfloat16)
    conv_sum = (
        convolve(first_input, conv_weight, near_ids, own_index, row_count, col_count) + step_embed
    )
    refined = (latent + conv_sum).astype(jnp.bfloat16)
    expand = up_weight.transpose(1, 0, 2).reshape(channels, 8 * out_channels)
    projected = jnp.dot(
        refined.reshape(slots_dev * edge_len**3, channels),
        expand,
        preferred_element_type=jnp.float32,
    )
    projected = projected.reshape(
        slots_dev, 2, half_len, 2, half_len, 2, half_len, 2, 2, 2, out_channels
    )
    projected = projected.transpose(0, 1, 3, 5, 2, 7, 4, 8, 6, 9, 10)
    payload = projected.reshape(slots_dev * 8, edge_len**3, out_channels).astype(jnp.bfloat16)
    item_shape = payload.shape[1:]
    send_cap = (8 * slots_dev + row_count - 1) // row_count
    is_valid = owner_ids >= 0
    target_row = jnp.where(is_valid, owner_ids // OCAP, 0)
    target_slot = jnp.where(is_valid, owner_ids % OCAP, -1)
    serial = jnp.arange(slots_dev * 8, dtype=jnp.int32)
    earlier = (
        (target_row[None, :] == target_row[:, None])
        & (serial[None, :] < serial[:, None])
        & is_valid[None, :]
    )
    ranked = jnp.sum(earlier.astype(jnp.int32), axis=1)
    position = jnp.where(is_valid, target_row * send_cap + ranked, row_count * send_cap)
    outgoing = (
        jnp.zeros((row_count * send_cap,) + item_shape, jnp.bfloat16)
        .at[position]
        .set(payload, mode="drop")
    )
    labels = (
        jnp.full((row_count * send_cap,), -1, jnp.int32).at[position].set(target_slot, mode="drop")
    )
    arrived, arrived_labels = (
        lax.all_to_all(
            outgoing.reshape((row_count, send_cap) + item_shape),
            "row",
            split_axis=0,
            concat_axis=0,
            tiled=True,
        ),
        lax.all_to_all(
            labels.reshape(row_count, send_cap), "row", split_axis=0, concat_axis=0, tiled=True
        ),
    )
    arrived = arrived.reshape((row_count * send_cap,) + item_shape)
    arrived_labels = arrived_labels.reshape(row_count * send_cap)
    placed = jnp.where(arrived_labels >= 0, arrived_labels, OCAP)
    upsampled = (
        jnp.zeros((OCAP, edge_len**3, out_channels), jnp.bfloat16)
        .at[placed]
        .set(arrived, mode="drop")
    )
    return upsampled.reshape(1, 1, 1, OCAP, edge_len, edge_len, edge_len, out_channels)


def solution(mesh):
    return jax.shard_map(
        body,
        mesh=mesh,
        in_specs=(
            P("depth", "row", "col", None, None, None, None, None),
            P("depth", "row", "col", None, None),
            P("depth", "row", "col", None, None),
            P(None, None, "row"),
            P(),
            P(),
        ),
        out_specs=P("depth", "row", "col", None, None, None, None, None),
        check_vma=False,
    )
```

profile of v0, /device:TPU:198, one launch (start us, length us, event | category | flops | bytes accessed | tf_op | source)
XLA Modules:
  0.0 205.4 jit_solution(4541175386371983872)
XLA Ops:
  6.5 0.0 all-gather.2.cloned.1.call-start
  6.5 0.7 all-gather.2.cloned.1.call-update
  7.3 1.9 fusion.5
  9.2 0.0 copy-start.4
  9.2 0.0 copy-start.3
  9.3 1.6 fusion.4
  10.9 0.9 fusion.56
  11.8 1.3 collective-permute-start
  13.1 5.2 %collective-permute-start.1 = (bf16[1,3,8,8,256]{4,1,3,2,0:T(4,128)(2,1)}, bf16[1,3,8,8,256]{4,1,3,2,0:T(4,128)(2,1)}, u32[]{:S(2)}, u32[]{:S(2)}) collective-permute-start(bf16[1,3,8,8,256]{4,1,3,2,0:T(4,128)(2,1)} %get-tuple-element.105), channel_id=1, source_target_pairs={{128,0},{256,128},{384,256},{129,1},{257,129},{385,257},{130,2},{2... | collective-permute-start | bytes 294920 | tf_op jit(solution)/shard_map/ppermute | solution.py:19
  18.3 0.2 fusion.55
  18.5 0.0 copy-start.2
  18.5 2.1 %collective-permute-start.2 = (bf16[1,3,8,8,256]{4,1,3,2,0:T(4,128)(2,1)S(1)}, bf16[1,3,8,8,256]{4,1,3,2,0:T(4,128)(2,1)}, u32[]{:S(2)}, u32[]{:S(2)}) collective-permute-start(bf16[1,3,8,8,256]{4,1,3,2,0:T(4,128)(2,1)S(1)} %get-tuple-element.100), channel_id=1, source_target_pairs={{0,8},{8,16},{16,24},{24,32},{32,40},{40,48},{48,56},{56,64},{64,7... | collective-permute-start | bytes 294920 | tf_op jit(solution)/shard_map/ppermute | solution.py:17
  20.6 1.3 collective-permute-start.3
  21.9 0.2 fusion.54
  22.1 5.5 %collective-permute-start.4 = (bf16[1,3,8,8,256]{4,1,3,2,0:T(4,128)(2,1)S(1)}, bf16[1,3,8,8,256]{4,1,3,2,0:T(4,128)(2,1)}, u32[]{:S(2)}, u32[]{:S(2)}) collective-permute-start(bf16[1,3,8,8,256]{4,1,3,2,0:T(4,128)(2,1)S(1)} %get-tuple-element.96), channel_id=1, source_target_pairs={{0,1},{1,2},{2,3},{3,4},{4,5},{5,6},{6,7},{8,9},{9,10},{10,11},{11... | collective-permute-start | bytes 294920 | tf_op jit(solution)/shard_map/ppermute | solution.py:17
  27.6 0.0 copy-done.4
  27.7 0.1 reshape.584
  27.7 0.1 reshape.583
  27.8 0.5 fusion.40
  28.3 0.2 convert_reduce_fusion
  28.6 0.8 scatter_custom_fusion
  29.3 0.7 all_to_all.9
  30.0 10.8 %all-to-all-start = ((s32[16,1,2]{2,1,0:T(1,128)}), s32[16,1,2]{2,1,0:T(1,128)S(1)}, u32[]{:S(2)}, u32[]{:S(2)}) async-start(s32[16,1,2]{2,1,0:T(1,128)} %bitcast.88), calls=%async_computation | async-start | bytes 16384 | tf_op jit(solution)/shard_map/all_to_all | solution.py:152
  40.8 2.0 scatter.45
  42.8 0.2 copy.48
  43.0 0.3 select_reduce_fusion
  43.3 0.0 collective-permute-done
  43.3 2.1 %collective-permute-start.5 = (bf16[1,3,8,8,256]{4,1,3,2,0:T(4,128)(2,1)S(1)}, bf16[1,3,8,8,256]{4,1,3,2,0:T(4,128)(2,1)S(1)}, u32[]{:S(2)}, u32[]{:S(2)}) collective-permute-start(bf16[1,3,8,8,256]{4,1,3,2,0:T(4,128)(2,1)S(1)} %get-tuple-element.97), channel_id=1, source_target_pairs={{1,0},{2,1},{3,2},{4,3},{5,4},{6,5},{7,6},{9,8},{10,9},{11,10},{12... | collective-permute-start | bytes 294920 | tf_op jit(solution)/shard_map/ppermute | solution.py:19
  45.4 0.0 copy-start.7
  45.4 1.3 convolution_convert_fusion.5
  46.7 0.7 constant_dynamic-update-slice_fusion.5
  47.4 0.0 collective-permute-done.1
  47.4 1.2 convolution_convert_fusion.4
  48.6 0.7 constant_dynamic-update-slice_fusion.4
  49.3 0.0 collective-permute-done.2
  49.3 1.2 convolution_convert_fusion.3
  50.5 0.7 constant_dynamic-update-slice_fusion.3
  51.2 0.0 collective-permute-done.3
  51.2 1.2 convolution_convert_fusion.2
  52.4 0.7 constant_dynamic-update-slice_fusion.2
  53.1 0.0 collective-permute-done.4
  53.1 1.2 convolution_convert_fusion.1
  54.3 0.7 constant_dynamic-update-slice_fusion.1
  55.0 0.0 collective-permute-done.5
  55.0 0.3 convolution_convert_fusion
  55.3 0.7 constant_dynamic-update-slice_fusion
  56.0 0.2 all-gather.2.cloned.1.call-done
  56.3 17.9 %fusion.6 = bf16[3,8,8,8,256]{4,0,3,2,1:T(4,128)(2,1)S(1)} fusion(bf16[3,10,10,10,256]{4,0,3,2,1:T(4,128)(2,1)} %constant_dynamic-update-slice_fusion, bf16[3,3,3,256,256]{3,4,2,1,0:T(8,128)(2,1)} %bitcast.89, f32[256]{0:T(256)S(1)} %copy-done.7, bf16[1,1,1,3,8,8,8,256]{7,6,5,4,3,2,1,0:T(8,128)(2,1)S(1)} %copy-done.1), kind=kOutput, calls=%fused_computation.19 | convolution fusion | flops 5437390848 | bytes 6648832 | tf_op jit(solution)/shard_map/conv_general_dilated | solution.py:86
  74.2 1.2 convert_bitcast_fusion
  75.4 3.4 %copy.50 = bf16[3,2,2,2,4,2,4,2,4,2,128]{10,9,8,7,6,5,4,3,2,1,0:T(2,128)(2,1)S(1)} copy(bf16[3,2,2,2,4,2,4,2,4,2,128]{10,8,9,7,5,3,6,2,4,1,0:T(4,128)(2,1)S(1)} %convert_bitcast_fusion) | data formatting | bytes 6291456 | tf_op jit(solution)/shard_map/convert_element_type | solution.py:122
  78.8 0.0 copy-start.6
  78.8 2.9 %broadcast_in_dim.62 = bf16[32,512,128]{2,1,0:T(8,128)(2,1)} broadcast(bf16[]{:T(256)} %constant.330.clone.1), dimensions={} | broadcast | bytes 4194306 | tf_op jit(solution)/shard_map/broadcast_in_dim | solution.py:137
  81.7 0.0 copy-done.6
  81.7 7.6 %scatter_fusion = bf16[32,512,128]{2,1,0:T(8,128)(2,1)} fusion(bf16[32,512,128]{2,1,0:T(8,128)(2,1)} %broadcast_in_dim.62, s32[24]{0:T(128)S(1)} %copy-done.6, bf16[24,512,128]{2,1,0:T(8,128)(2,1)S(1)} %bitcast.73), kind=kCustom, calls=%fused_computation.1 | custom fusion | bytes 9437280 | tf_op jit(solution)/shard_map/scatter | solution.py:139
  89.3 0.0 all-to-all-done
  89.3 7.0 %all-to-all-start.1 = ((bf16[16,2,512,128]{3,2,1,0:T(8,128)(2,1)}), bf16[16,2,512,128]{3,2,1,0:T(8,128)(2,1)}, u32[]{:S(2)}, u32[]{:S(2)}) async-start(bf16[16,2,512,128]{3,2,1,0:T(8,128)(2,1)} %bitcast.72), calls=%async_computation.1 | async-start | bytes 8388608 | tf_op jit(solution)/shard_map/all_to_all | solution.py:145
  96.3 0.5 broadcast.496
  96.8 0.7 reduce.31
  97.5 0.1 reshape.585
  97.6 93.0 %all-to-all-done.1 = bf16[16,2,512,128]{3,2,1,0:T(8,128)(2,1)} async-done(((bf16[16,2,512,128]{3,2,1,0:T(8,128)(2,1)}), bf16[16,2,512,128]{3,2,1,0:T(8,128)(2,1)}, u32[]{:S(2)}, u32[]{:S(2)}) %all-to-all-start.1) | async-done | bytes 4194336 | tf_op jit(solution)/shard_map/all_to_all | solution.py:145
  190.6 0.4 broadcast_in_dim.31
  191.0 6.3 %scatter_fusion.1 = bf16[16,512,128]{2,1,0:T(8,128)(2,1)S(1)} fusion(bf16[16,512,128]{2,1,0:T(8,128)(2,1)S(1)} %broadcast_in_dim.31, s32[32]{0:T(128)S(1)} %fusion.44, bf16[32,512,128]{2,1,0:T(8,128)(2,1)} %bitcast.42), kind=kCustom, calls=%fused_computation.2 | custom fusion | bytes 12583040 | tf_op jit(solution)/shard_map/scatter | solution.py:162
  197.3 0.0 copy-start
  197.3 1.3 copy-done
  (13 shorter events, 0.1 us)
Async XLA Ops:
  6.5 2.7 %copy-start.1 = (bf16[1,1,1,3,8,8,8,256]{7,6,5,4,3,2,1,0:T(8,128)(2,1)S(1)}, bf16[1,1,1,3,8,8,8,256]{7,6,5,4,3,2,1,0:T(8,128)(2,1)}, u32[]{:S(2)}) copy-start(bf16[1,1,1,3,8,8,8,256]{7,6,5,4,3,2,1,0:T(8,128)(2,1)} %param.20) | copy-start | bytes 2359300
  6.5 49.7 %all-gather.2.cloned.1.call-start = ((), (), s32[]{:S(2)}) async-start(), calls=%async_computation.2 | async-start | bytes 3760128 | tf_op jit(solution)/shard_map/all_gather | solution.py:84
  9.2 18.4 %copy-start.4 = (s32[1,1,1,3,8]{4,2,3,1,0:T(1,128)S(1)}, s32[1,1,1,3,8]{4,2,3,1,0:T(1,128)}, u32[]{:S(2)}) copy-start(s32[1,1,1,3,8]{4,2,3,1,0:T(1,128)} %param.22) | copy-start | bytes 292
  9.2 31.6 %copy-start.3 = (s32[1,1,1,3,6]{4,2,3,1,0:T(1,128)S(1)}, s32[1,1,1,3,6]{4,2,3,1,0:T(1,128)}, u32[]{:S(2)}) copy-start(s32[1,1,1,3,6]{4,2,3,1,0:T(1,128)} %param.21) | copy-start | bytes 220
  11.8 31.5 %collective-permute-start = (bf16[1,3,8,8,256]{4,1,3,2,0:T(4,128)(2,1)}, bf16[1,3,8,8,256]{4,1,3,2,0:T(4,128)(2,1)}, u32[]{:S(2)}, u32[]{:S(2)}) collective-permute-start(bf16[1,3,8,8,256]{4,1,3,2,0:T(4,128)(2,1)} %get-tuple-element.104), channel_id=1, source_target_pairs={{0,128},{128,256},{256,384},{1,129},{129,257},{257,385},{2,130},{1... | collective-permute-start | bytes 294920 | tf_op jit(solution)/shard_map/ppermute | solution.py:17
  13.1 34.4 %collective-permute-start.1 = (bf16[1,3,8,8,256]{4,1,3,2,0:T(4,128)(2,1)}, bf16[1,3,8,8,256]{4,1,3,2,0:T(4,128)(2,1)}, u32[]{:S(2)}, u32[]{:S(2)}) collective-permute-start(bf16[1,3,8,8,256]{4,1,3,2,0:T(4,128)(2,1)} %get-tuple-element.105), channel_id=1, source_target_pairs={{128,0},{256,128},{384,256},{129,1},{257,129},{385,257},{130,2},{2... | collective-permute-start | bytes 294920 | tf_op jit(solution)/shard_map/ppermute | solution.py:19
  18.5 24.3 %copy-start.2 = (bf16[8,256,128]{2,1,0:T(8,128)(2,1)S(1)}, bf16[8,256,128]{2,1,0:T(8,128)(2,1)}, u32[]{:S(2)}) copy-start(bf16[8,256,128]{2,1,0:T(8,128)(2,1)} %param.25) | copy-start | bytes 1572868
  18.5 30.8 %collective-permute-start.2 = (bf16[1,3,8,8,256]{4,1,3,2,0:T(4,128)(2,1)S(1)}, bf16[1,3,8,8,256]{4,1,3,2,0:T(4,128)(2,1)}, u32[]{:S(2)}, u32[]{:S(2)}) collective-permute-start(bf16[1,3,8,8,256]{4,1,3,2,0:T(4,128)(2,1)S(1)} %get-tuple-element.100), channel_id=1, source_target_pairs={{0,8},{8,16},{16,24},{24,32},{32,40},{40,48},{48,56},{56,64},{64,7... | collective-permute-start | bytes 294920 | tf_op jit(solution)/shard_map/ppermute | solution.py:17
  20.6 30.6 %collective-permute-start.3 = (bf16[1,3,8,8,256]{4,1,3,2,0:T(4,128)(2,1)S(1)}, bf16[1,3,8,8,256]{4,1,3,2,0:T(4,128)(2,1)}, u32[]{:S(2)}, u32[]{:S(2)}) collective-permute-start(bf16[1,3,8,8,256]{4,1,3,2,0:T(4,128)(2,1)S(1)} %get-tuple-element.101), channel_id=1, source_target_pairs={{8,0},{16,8},{24,16},{32,24},{40,32},{48,40},{56,48},{64,56},{72,6... | collective-permute-start | bytes 294920 | tf_op jit(solution)/shard_map/ppermute | solution.py:19
  22.1 31.0 %collective-permute-start.4 = (bf16[1,3,8,8,256]{4,1,3,2,0:T(4,128)(2,1)S(1)}, bf16[1,3,8,8,256]{4,1,3,2,0:T(4,128)(2,1)}, u32[]{:S(2)}, u32[]{:S(2)}) collective-permute-start(bf16[1,3,8,8,256]{4,1,3,2,0:T(4,128)(2,1)S(1)} %get-tuple-element.96), channel_id=1, source_target_pairs={{0,1},{1,2},{2,3},{3,4},{4,5},{5,6},{6,7},{8,9},{9,10},{10,11},{11... | collective-permute-start | bytes 294920 | tf_op jit(solution)/shard_map/ppermute | solution.py:17
  28.5 12.3 %copy-start.5 = (s32[24]{0:T(128)}, s32[24]{0:T(128)S(1)}, u32[]{:S(2)}) copy-start(s32[24]{0:T(128)S(1)} %fusion.43) | copy-start | bytes 292
  30.0 59.2 %all-to-all-start = ((s32[16,1,2]{2,1,0:T(1,128)}), s32[16,1,2]{2,1,0:T(1,128)S(1)}, u32[]{:S(2)}, u32[]{:S(2)}) async-start(s32[16,1,2]{2,1,0:T(1,128)} %bitcast.88), calls=%async_computation | async-start | bytes 16384 | tf_op jit(solution)/shard_map/all_to_all | solution.py:152
  43.3 11.7 %collective-permute-start.5 = (bf16[1,3,8,8,256]{4,1,3,2,0:T(4,128)(2,1)S(1)}, bf16[1,3,8,8,256]{4,1,3,2,0:T(4,128)(2,1)S(1)}, u32[]{:S(2)}, u32[]{:S(2)}) collective-permute-start(bf16[1,3,8,8,256]{4,1,3,2,0:T(4,128)(2,1)S(1)} %get-tuple-element.97), channel_id=1, source_target_pairs={{1,0},{2,1},{3,2},{4,3},{5,4},{6,5},{7,6},{9,8},{10,9},{11,10},{12... | collective-permute-start | bytes 294920 | tf_op jit(solution)/shard_map/ppermute | solution.py:19
  45.4 10.8 %copy-start.7 = (f32[256]{0:T(256)S(1)}, f32[256]{0:T(256)}, u32[]{:S(2)}) copy-start(f32[256]{0:T(256)} %param.24) | copy-start | bytes 3076
  78.8 2.9 %copy-start.6 = (s32[24]{0:T(128)S(1)}, s32[24]{0:T(128)}, u32[]{:S(2)}) copy-start(s32[24]{0:T(128)} %copy-done.5) | copy-start | bytes 292
  89.3 101.3 %all-to-all-start.1 = ((bf16[16,2,512,128]{3,2,1,0:T(8,128)(2,1)}), bf16[16,2,512,128]{3,2,1,0:T(8,128)(2,1)}, u32[]{:S(2)}, u32[]{:S(2)}) async-start(bf16[16,2,512,128]{3,2,1,0:T(8,128)(2,1)} %bitcast.72), calls=%async_computation.1 | async-start | bytes 8388608 | tf_op jit(solution)/shard_map/all_to_all | solution.py:145
  197.3 1.3 copy-start
Sparse Core Ops, SparseCore 0:
  9.5 46.7 all-gather.1
where the time goes:
time: 206 us; the launch traced here: 205 us
  waiting for transfers between devices  94 us (46%)
  starting transfers between devices  35.2 us (17%)
  local copies, waits for them, and re-layouts  31.9 us (15%)
  matrix products  25.4 us (12%)
  between operations  13.7 us (7%)
  other arithmetic  5.3 us (3%)
    all_to_all x1, waiting for transfers between devices, body(): lax.all_to_all(outgoing.reshape((row_count, send_cap) + item_shape), 'row...  93 us
    conv_general_dilated x1, matrix products, convolve(): lax.conv_general_dilated(padded, kernel, (1, 1, 1), 'VALID', dimension_nu...  17.9 us
    all_to_all x1, starting transfers between devices, body(): lax.all_to_all(labels.reshape(row_count, send_cap), 'row', split_axis=0,...  10.8 us
    ppermute x3, starting transfers between devices, with_halo(): lax.ppermute(tail, axis, [(i, (i + 1) % count) for i in range(ends)])  8.86 us
    ppermute x3, starting transfers between devices, with_halo(): lax.ppermute(head, axis, [((i + 1) % count, i) for i in range(ends)])  8.57 us
    scatter x1, local copies, waits for them, and re-layouts, body(): outgoing = jnp.zeros((row_count * send_cap,) + item_shape, jnp.bfloat16)....  7.56 us
    all_to_all x1, starting transfers between devices, body(): lax.all_to_all(outgoing.reshape((row_count, send_cap) + item_shape), 'row...  7 us
    dot_general x6, matrix products, borrowed(): picked = jnp.dot(picker, stacked, preferred_element_type=jnp.float32)  6.28 us
  transfers between devices with their start and end apart: 9, of which 2 were waited for; matrix products, arithmetic and copies ran while one was open for 26% of the time, Pallas kernels for 0%

commit v1 on v0

--- a/solution.py
+++ b/solution.py
@@ -81,7 +81,9 @@
 def convolve(source, weight, near_ids, own_index, row_count, col_count):
     channels = source.shape[-1]
     padded = padded_field(source, near_ids, own_index, row_count, col_count)
-    weight_piece = lax.all_gather(weight, "row", axis=2, tiled=True)
+    weight_piece = jnp.concatenate(
+        lax.all_to_all(jnp.stack([weight] * lax.axis_size("row")), "row", 0, 0), axis=2
+    )
     kernel = weight_piece.reshape(3, 3, 3, channels, weight_piece.shape[2])
     return lax.conv_general_dilated(
         padded,

time: 206 us -> 249 us (1.21)
  the two profiles are of different devices: /device:TPU:198 before, /device:TPU:1 now
where the time goes in v1:
time: 249 us; the launch traced here: 248 us
  waiting for transfers between devices  137 us (55%)
  starting transfers between devices  41.2 us (17%)
  local copies, waits for them, and re-layouts  40.6 us (16%)
  matrix products  23.5 us (9%)
  other arithmetic  5.42 us (2%)
    all_to_all x1, waiting for transfers between devices, body(): lax.all_to_all(outgoing.reshape((row_count, send_cap) + item_shape), 'row...  92.3 us
    ppermute x3, waiting for transfers between devices, with_halo(): lax.ppermute(tail, axis, [(i, (i + 1) % count) for i in range(ends)])  44.6 us
    conv_general_dilated x1, matrix products, convolve(): lax.conv_general_dilated(padded, kernel, (1, 1, 1), 'VALID', dimension_nu...  15.9 us
    all_to_all x1, starting transfers between devices, convolve(): lax.all_to_all(jnp.stack([weight] * lax.axis_size('row')), 'row', 0, 0)  10.4 us
    ppermute x3, starting transfers between devices, with_halo(): lax.ppermute(tail, axis, [(i, (i + 1) % count) for i in range(ends)])  10.4 us
    all_to_all x1, starting transfers between devices, body(): lax.all_to_all(labels.reshape(row_count, send_cap), 'row', split_axis=0,...  8.21 us
    all_to_all x1, starting transfers between devices, body(): lax.all_to_all(outgoing.reshape((row_count, send_cap) + item_shape), 'row...  7.63 us
    scatter x1, local copies, waits for them, and re-layouts, body(): outgoing = jnp.zeros((row_count * send_cap,) + item_shape, jnp.bfloat16)....  6.85 us
  transfers between devices with their start and end apart: 9, of which 2 were waited for; matrix products, arithmetic and copies ran while one was open for 23% of the time, Pallas kernels for 0%

profile of v1, /device:TPU:1, one launch (start us, length us, event | category | flops | bytes accessed | tf_op | source)
XLA Modules:
  0.0 247.9 jit_solution(7061898322979533045)
XLA Ops:
  0.0 2.9 %stack.2 = bf16[16,27,256,16]{2,3,1,0:T(8,128)(2,1)} broadcast(bf16[27,256,16]{1,2,0:T(8,128)(2,1)} %param.23), dimensions={1,2,3} | broadcast | bytes 3760128 | tf_op jit(solution)/shard_map/stack | solution.py:85
  2.9 10.4 %all-to-all-start.1 = ((bf16[16,27,256,16]{2,3,1,0:T(8,128)(2,1)}), bf16[16,27,256,16]{2,3,1,0:T(8,128)(2,1)S(1)}, u32[]{:S(2)}, u32[]{:S(2)}) async-start(bf16[16,27,256,16]{2,3,1,0:T(8,128)(2,1)} %stack.2), calls=%async_computation.1 | async-start | bytes 7077888 | tf_op jit(solution)/shard_map/all_to_all | solution.py:85
  13.3 2.0 fusion.5
  15.4 0.0 copy-start.10
  15.4 0.0 copy-start.9
  15.4 1.6 fusion.4
  17.1 1.1 fusion.56
  18.2 2.0 collective-permute-start
  20.2 1.3 collective-permute-start.1
  21.5 0.9 fusion.55
  22.4 3.8 %collective-permute-start.2 = (bf16[1,3,8,8,256]{4,1,3,2,0:T(4,128)(2,1)}, bf16[1,3,8,8,256]{4,1,3,2,0:T(4,128)(2,1)}, u32[]{:S(2)}, u32[]{:S(2)}) collective-permute-start(bf16[1,3,8,8,256]{4,1,3,2,0:T(4,128)(2,1)} %get-tuple-element.100), channel_id=1, source_target_pairs={{0,8},{8,16},{16,24},{24,32},{32,40},{40,48},{48,56},{56,64},{64,7... | collective-permute-start | bytes 294920 | tf_op jit(solution)/shard_map/ppermute | solution.py:17
  26.2 1.9 collective-permute-start.3
  28.2 0.9 fusion.54
  29.1 4.6 %collective-permute-start.4 = (bf16[1,3,8,8,256]{4,1,3,2,0:T(4,128)(2,1)}, bf16[1,3,8,8,256]{4,1,3,2,0:T(4,128)(2,1)}, u32[]{:S(2)}, u32[]{:S(2)}) collective-permute-start(bf16[1,3,8,8,256]{4,1,3,2,0:T(4,128)(2,1)} %get-tuple-element.96), channel_id=1, source_target_pairs={{0,1},{1,2},{2,3},{3,4},{4,5},{5,6},{6,7},{8,9},{9,10},{10,11},{11... | collective-permute-start | bytes 294920 | tf_op jit(solution)/shard_map/ppermute | solution.py:17
  33.8 0.1 reshape.586
  33.9 0.1 reshape.585
  33.9 3.2 %scatter.45 = bf16[3,10,10,10,256]{4,0,3,2,1:T(4,128)(2,1)} pad(bf16[3,8,8,8,256]{4,0,3,2,1:T(4,128)(2,1)} %copy-done.1, bf16[]{:T(256)} %constant.330.clone.1), padding=0_0x1_1x1_1x1_1x0_0 | pad | bytes 2322434 | tf_op jit(solution)/shard_map/scatter | solution.py:71
  37.1 2.0 copy.47
  39.2 0.6 fusion.40
  39.7 0.2 convert_reduce_fusion
  39.9 0.8 scatter_custom_fusion
  40.7 0.7 all_to_all.12
  41.4 0.3 select_reduce_fusion
  41.7 0.0 collective-permute-done
  41.7 1.3 collective-permute-start.5
  43.0 1.2 convolution_convert_fusion.5
  44.3 0.7 constant_dynamic-update-slice_fusion.5
  45.0 0.0 collective-permute-done.1
  45.0 1.2 convolution_convert_fusion.4
  46.2 0.7 constant_dynamic-update-slice_fusion.4
  46.9 44.6 %collective-permute-done.2 = bf16[1,3,8,8,256]{4,1,3,2,0:T(4,128)(2,1)} collective-permute-done((bf16[1,3,8,8,256]{4,1,3,2,0:T(4,128)(2,1)}, bf16[1,3,8,8,256]{4,1,3,2,0:T(4,128)(2,1)}, u32[]{:S(2)}, u32[]{:S(2)}) %collective-permute-start.2) | collective-permute-done | bytes 98336 | tf_op jit(solution)/shard_map/ppermute | solution.py:17
  91.6 1.2 convolution_convert_fusion.3
  92.8 0.7 constant_dynamic-update-slice_fusion.3
  93.5 0.0 collective-permute-done.3
  93.5 1.2 convolution_convert_fusion.2
  94.7 0.7 constant_dynamic-update-slice_fusion.2
  95.4 0.0 collective-permute-done.4
  95.4 1.2 convolution_convert_fusion.1
  96.6 0.7 constant_dynamic-update-slice_fusion.1
  97.3 0.0 collective-permute-done.5
  97.3 0.3 convolution_convert_fusion
  97.6 0.7 constant_dynamic-update-slice_fusion
  98.3 0.0 all-to-all-done.1
  98.3 8.2 %all-to-all-start = ((s32[16,1,2]{2,1,0:T(1,128)}), s32[16,1,2]{2,1,0:T(1,128)S(1)}, u32[]{:S(2)}, u32[]{:S(2)}) async-start(s32[16,1,2]{2,1,0:T(1,128)} %bitcast.2), calls=%async_computation | async-start | bytes 16384 | tf_op jit(solution)/shard_map/all_to_all | solution.py:154
  106.5 0.0 copy-start.4
  106.6 0.0 copy-start.11
  106.6 0.4 copy.46
  107.0 0.7 copy-done.3
  107.7 0.7 copy-done.4
  108.4 15.9 %fusion.6 = bf16[3,8,8,8,256]{4,0,3,2,1:T(4,128)(2,1)S(1)} fusion(bf16[3,10,10,10,256]{4,0,3,2,1:T(4,128)(2,1)S(1)} %copy-done.4, bf16[3,3,3,256,256]{3,4,2,1,0:T(8,128)(2,1)S(1)} %bitcast.75, f32[256]{0:T(256)S(1)} %copy-done.11, bf16[1,1,1,3,8,8,8,256]{7,6,5,4,3,2,1,0:T(8,128)(2,1)S(1)} %copy-done.3), kind=kOutput, calls=%fused_computation.19 | convolution fusion | flops 5437390848 | bytes 6648832 | tf_op jit(solution)/shard_map/conv_general_dilated | solution.py:88
  124.3 1.2 convert_bitcast_fusion
  125.5 3.4 %copy.49 = bf16[3,2,2,2,4,2,4,2,4,2,128]{10,9,8,7,6,5,4,3,2,1,0:T(2,128)(2,1)S(1)} copy(bf16[3,2,2,2,4,2,4,2,4,2,128]{10,8,9,7,5,3,6,2,4,1,0:T(4,128)(2,1)S(1)} %convert_bitcast_fusion) | data formatting | bytes 6291456 | tf_op jit(solution)/shard_map/convert_element_type | solution.py:124
  128.9 2.9 %broadcast_in_dim.62 = bf16[32,512,128]{2,1,0:T(8,128)(2,1)} broadcast(bf16[]{:T(256)} %constant.330.clone.1), dimensions={} | broadcast | bytes 4194306 | tf_op jit(solution)/shard_map/broadcast_in_dim | solution.py:139
  131.8 6.9 %scatter_fusion = bf16[32,512,128]{2,1,0:T(8,128)(2,1)} fusion(bf16[32,512,128]{2,1,0:T(8,128)(2,1)} %broadcast_in_dim.62, s32[24]{0:T(128)S(1)} %fusion.43, bf16[24,512,128]{2,1,0:T(8,128)(2,1)S(1)} %bitcast.74), kind=kCustom, calls=%fused_computation.1 | custom fusion | bytes 9437280 | tf_op jit(solution)/shard_map/scatter | solution.py:141
  138.7 0.0 all-to-all-done
  138.7 7.6 %all-to-all-start.2 = ((bf16[16,2,512,128]{3,2,1,0:T(8,128)(2,1)}), bf16[16,2,512,128]{3,2,1,0:T(8,128)(2,1)}, u32[]{:S(2)}, u32[]{:S(2)}) async-start(bf16[16,2,512,128]{3,2,1,0:T(8,128)(2,1)} %bitcast.73), calls=%async_computation.2 | async-start | bytes 8388608 | tf_op jit(solution)/shard_map/all_to_all | solution.py:147
  146.3 0.5 broadcast.498
  146.8 0.7 reduce.31
  147.5 0.1 reshape.587
  147.6 92.3 %all-to-all-done.2 = bf16[16,2,512,128]{3,2,1,0:T(8,128)(2,1)} async-done(((bf16[16,2,512,128]{3,2,1,0:T(8,128)(2,1)}), bf16[16,2,512,128]{3,2,1,0:T(8,128)(2,1)}, u32[]{:S(2)}, u32[]{:S(2)}) %all-to-all-start.2) | async-done | bytes 4194336 | tf_op jit(solution)/shard_map/all_to_all | solution.py:147
  239.9 0.4 broadcast_in_dim.31
  240.3 6.3 %scatter_fusion.1 = bf16[16,512,128]{2,1,0:T(8,128)(2,1)S(1)} fusion(bf16[16,512,128]{2,1,0:T(8,128)(2,1)S(1)} %broadcast_in_dim.31, s32[32]{0:T(128)S(1)} %fusion.44, bf16[32,512,128]{2,1,0:T(8,128)(2,1)} %bitcast.43), kind=kCustom, calls=%fused_computation.2 | custom fusion | bytes 12583040 | tf_op jit(solution)/shard_map/scatter | solution.py:164
  246.6 0.0 copy-start
  246.6 1.3 copy-done
  (22 shorter events, 0.1 us)
Async XLA Ops:
  2.9 95.4 %all-to-all-start.1 = ((bf16[16,27,256,16]{2,3,1,0:T(8,128)(2,1)}), bf16[16,27,256,16]{2,3,1,0:T(8,128)(2,1)S(1)}, u32[]{:S(2)}, u32[]{:S(2)}) async-start(bf16[16,27,256,16]{2,3,1,0:T(8,128)(2,1)} %stack.2), calls=%async_computation.1 | async-start | bytes 7077888 | tf_op jit(solution)/shard_map/all_to_all | solution.py:85
  13.3 2.0 copy-start.2
  15.4 18.4 %copy-start.10 = (s32[1,1,1,3,8]{4,2,3,1,0:T(1,128)S(1)}, s32[1,1,1,3,8]{4,2,3,1,0:T(1,128)}, u32[]{:S(2)}) copy-start(s32[1,1,1,3,8]{4,2,3,1,0:T(1,128)} %param.22) | copy-start | bytes 292
  15.4 18.5 %copy-start.9 = (s32[1,1,1,3,6]{4,2,3,1,0:T(1,128)S(1)}, s32[1,1,1,3,6]{4,2,3,1,0:T(1,128)}, u32[]{:S(2)}) copy-start(s32[1,1,1,3,6]{4,2,3,1,0:T(1,128)} %param.21) | copy-start | bytes 220
  17.1 11.1 %copy-start.1 = (bf16[3,8,8,8,256]{4,0,3,2,1:T(4,128)(2,1)}, bf16[3,8,8,8,256]{4,0,3,2,1:T(4,128)(2,1)S(1)}, u32[]{:S(2)}) copy-start(bf16[3,8,8,8,256]{4,0,3,2,1:T(4,128)(2,1)S(1)} %fusion.4) | copy-start | bytes 2359300
  18.2 23.5 %collective-permute-start = (bf16[1,3,8,8,256]{4,1,3,2,0:T(4,128)(2,1)}, bf16[1,3,8,8,256]{4,1,3,2,0:T(4,128)(2,1)}, u32[]{:S(2)}, u32[]{:S(2)}) collective-permute-start(bf16[1,3,8,8,256]{4,1,3,2,0:T(4,128)(2,1)} %get-tuple-element.104), channel_id=1, source_target_pairs={{0,128},{128,256},{256,384},{1,129},{129,257},{257,385},{2,130},{1... | collective-permute-start | bytes 294920 | tf_op jit(solution)/shard_map/ppermute | solution.py:17
  20.2 24.8 %collective-permute-start.1 = (bf16[1,3,8,8,256]{4,1,3,2,0:T(4,128)(2,1)}, bf16[1,3,8,8,256]{4,1,3,2,0:T(4,128)(2,1)}, u32[]{:S(2)}, u32[]{:S(2)}) collective-permute-start(bf16[1,3,8,8,256]{4,1,3,2,0:T(4,128)(2,1)} %get-tuple-element.105), channel_id=1, source_target_pairs={{128,0},{256,128},{384,256},{129,1},{257,129},{385,257},{130,2},{2... | collective-permute-start | bytes 294920 | tf_op jit(solution)/shard_map/ppermute | solution.py:19
  22.4 69.1 %collective-permute-start.2 = (bf16[1,3,8,8,256]{4,1,3,2,0:T(4,128)(2,1)}, bf16[1,3,8,8,256]{4,1,3,2,0:T(4,128)(2,1)}, u32[]{:S(2)}, u32[]{:S(2)}) collective-permute-start(bf16[1,3,8,8,256]{4,1,3,2,0:T(4,128)(2,1)} %get-tuple-element.100), channel_id=1, source_target_pairs={{0,8},{8,16},{16,24},{24,32},{32,40},{40,48},{48,56},{56,64},{64,7... | collective-permute-start | bytes 294920 | tf_op jit(solution)/shard_map/ppermute | solution.py:17
  26.2 67.3 %collective-permute-start.3 = (bf16[1,3,8,8,256]{4,1,3,2,0:T(4,128)(2,1)}, bf16[1,3,8,8,256]{4,1,3,2,0:T(4,128)(2,1)}, u32[]{:S(2)}, u32[]{:S(2)}) collective-permute-start(bf16[1,3,8,8,256]{4,1,3,2,0:T(4,128)(2,1)} %get-tuple-element.101), channel_id=1, source_target_pairs={{8,0},{16,8},{24,16},{32,24},{40,32},{48,40},{56,48},{64,56},{72,6... | collective-permute-start | bytes 294920 | tf_op jit(solution)/shard_map/ppermute | solution.py:19
  29.1 66.3 %collective-permute-start.4 = (bf16[1,3,8,8,256]{4,1,3,2,0:T(4,128)(2,1)}, bf16[1,3,8,8,256]{4,1,3,2,0:T(4,128)(2,1)}, u32[]{:S(2)}, u32[]{:S(2)}) collective-permute-start(bf16[1,3,8,8,256]{4,1,3,2,0:T(4,128)(2,1)} %get-tuple-element.96), channel_id=1, source_target_pairs={{0,1},{1,2},{2,3},{3,4},{4,5},{5,6},{6,7},{8,9},{9,10},{10,11},{11... | collective-permute-start | bytes 294920 | tf_op jit(solution)/shard_map/ppermute | solution.py:17
  41.4 52.1 %copy-start.8 = (bf16[3,8,1,8,256]{4,0,3,2,1:T(4,128)(2,1)S(1)}, bf16[3,8,1,8,256]{4,0,3,2,1:T(4,128)(2,1)}, u32[]{:S(2)}) copy-start(bf16[3,8,1,8,256]{4,0,3,2,1:T(4,128)(2,1)} %get-tuple-element.99) | copy-start | bytes 294916
  41.4 54.0 %copy-start.7 = (bf16[3,8,8,1,256]{4,0,3,2,1:T(4,128)(2,1)S(1)}, bf16[3,8,8,1,256]{4,0,3,2,1:T(4,128)(2,1)}, u32[]{:S(2)}) copy-start(bf16[3,8,8,1,256]{4,0,3,2,1:T(4,128)(2,1)} %get-tuple-element.98) | copy-start | bytes 294916
  41.4 55.9 %copy-start.6 = (bf16[3,8,8,1,256]{4,0,3,2,1:T(4,128)(2,1)S(1)}, bf16[3,8,8,1,256]{4,0,3,2,1:T(4,128)(2,1)}, u32[]{:S(2)}) copy-start(bf16[3,8,8,1,256]{4,0,3,2,1:T(4,128)(2,1)} %get-tuple-element.95) | copy-start | bytes 294916
  41.7 55.6 %collective-permute-start.5 = (bf16[1,3,8,8,256]{4,1,3,2,0:T(4,128)(2,1)}, bf16[1,3,8,8,256]{4,1,3,2,0:T(4,128)(2,1)S(1)}, u32[]{:S(2)}, u32[]{:S(2)}) collective-permute-start(bf16[1,3,8,8,256]{4,1,3,2,0:T(4,128)(2,1)} %get-tuple-element.97), channel_id=1, source_target_pairs={{1,0},{2,1},{3,2},{4,3},{5,4},{6,5},{7,6},{9,8},{10,9},{11,10},{12... | collective-permute-start | bytes 294920 | tf_op jit(solution)/shard_map/ppermute | solution.py:19
  98.3 40.4 %all-to-all-start = ((s32[16,1,2]{2,1,0:T(1,128)}), s32[16,1,2]{2,1,0:T(1,128)S(1)}, u32[]{:S(2)}, u32[]{:S(2)}) async-start(s32[16,1,2]{2,1,0:T(1,128)} %bitcast.2), calls=%async_computation | async-start | bytes 16384 | tf_op jit(solution)/shard_map/all_to_all | solution.py:154
  106.5 1.1 copy-start.3
  106.5 1.8 copy-start.4
  106.6 1.8 copy-start.11
  108.4 15.9 %copy-start.5 = (bf16[8,256,128]{1,2,0:T(8,128)(2,1)S(1)}, bf16[8,256,128]{1,2,0:T(8,128)(2,1)}, u32[]{:S(2)}) copy-start(bf16[8,256,128]{1,2,0:T(8,128)(2,1)} %copy.47) | copy-start | bytes 1572868
  138.7 101.2 %all-to-all-start.2 = ((bf16[16,2,512,128]{3,2,1,0:T(8,128)(2,1)}), bf16[16,2,512,128]{3,2,1,0:T(8,128)(2,1)}, u32[]{:S(2)}, u32[]{:S(2)}) async-start(bf16[16,2,512,128]{3,2,1,0:T(8,128)(2,1)} %bitcast.73), calls=%async_computation.2 | async-start | bytes 8388608 | tf_op jit(solution)/shard_map/all_to_all | solution.py:147
  246.6 1.3 copy-start
